TPU v7x, 32 devices: a whole 2x2x4 slice. The times are simulated.
32 devices in a mesh: blk: 8 (over y, x, core), rep: 4 (over z).
Axes of the slice: x: 2, y: 2, z: 4, core: 2. Of those that a mesh axis runs over, the one named last changes fastest.
Arguments:
- stale: bfloat16 [4096, 512], P(('blk', 'rep')), may hold values from -6 to 6
- w_self: bfloat16 [512, 512], replicated, may hold values from -0.25 to 0.25
- w_neigh: bfloat16 [512, 512], replicated, may hold values from -6 to 6
- tile_weights: bfloat16 [8, 4, 8, 3, 128, 128], P('blk', 'rep'), may hold values from 0 to 4, as said below
- tile_pos: int32 [8, 4, 8, 3], P('blk', 'rep'), may hold values from 0 to 3, as said below
- tile_counts: int32 [8, 4, 8], P('blk', 'rep'), may hold values from 0 to 3, as said below
Outputs:
- refreshed: bfloat16 [4096, 512], P(('blk', 'rep'))
Inputs may be any that keep to these rules, and one draw needn't show every extreme that they name: `tile_weights`: non-negative edge weights. `tile_pos`: distinct within the live head of every list. `tile_counts`: every device has one full list.
All inputs are finite; a program needn't handle non-finite values.
Results may differ from a plain program's by a relative error of at most 0.013.
Values may be sent and summed in bfloat16 or wider, within the bound.
A program may use at most 64 MiB of HBM per device.

v0:
```python
import jax
import jax.numpy as jnp
from jax import lax
from jax.sharding import PartitionSpec as P


def passed_along(value, axis, steps):
    count = lax.axis_size(axis)
    pairs = [(source, (source + steps) % count) for source in range(count)]
    return lax.ppermute(value, axis, pairs)


def on_device(stale, w_self, w_neigh, tile_weights, tile_pos, tile_counts):
    blocks = lax.axis_size("blk")
    members = lax.axis_size("rep")
    my_group = lax.axis_index("blk")
    weights = tile_weights[0, 0]
    places = tile_pos[0, 0]
    counts = tile_counts[0, 0]
    own_count, width = stale.shape
    tile_size = weights.shape[-1]
    capacity = weights.shape[1]
    col_tiles = own_count // tile_size
    group_rows = own_count * members
    row_tiles = group_rows // tile_size

    def take_tiles(totals, degree, source_block, shard_id, active):
        shard_tiles = lax.dynamic_index_in_dim(weights, shard_id, 0, keepdims=False)
        shard_places = lax.dynamic_index_in_dim(places, shard_id, 0, keepdims=False)
        live_count = lax.dynamic_index_in_dim(counts, shard_id, 0, keepdims=False) * active
        live_mask = (jnp.arange(capacity) < live_count).astype(jnp.bfloat16)
        tiles = shard_tiles * live_mask[:, None, None]
        column = shard_places % col_tiles
        row_tile = shard_places // col_tiles
        picked = jnp.take(source_block.reshape(col_tiles, tile_size, width), column, axis=0)
        products = jnp.einsum("kij,kjd->kid", tiles, picked, preferred_element_type=jnp.float32)
        totals = (
            totals.reshape(row_tiles, tile_size, width)
            .at[row_tile]
            .add(products)
            .reshape(group_rows, width)
        )
        row_sums = jnp.sum(tiles.astype(jnp.float32), axis=2)
        degree = degree.reshape(row_tiles, tile_size).at[row_tile].add(row_sums).reshape(group_rows)
        return (totals, degree)

    totals = jnp.zeros((group_rows, width), jnp.float32)
    degree = jnp.zeros((group_rows,), jnp.float32)
    totals, degree = take_tiles(totals, degree, stale, my_group, 1)
    half_cycle = blocks // 2

    def turn_double(turn, running):
        part_sum, part_deg, ahead_block, behind = running
        ahead_block = passed_along(ahead_block, "blk", 1)
        behind = passed_along(behind, "blk", -1)
        part_sum, part_deg = take_tiles(
            part_sum, part_deg, ahead_block, (my_group - turn) % blocks, 1
        )
        active = jnp.where(turn < half_cycle, 1, 0).astype(jnp.int32)
        part_sum, part_deg = take_tiles(
            part_sum, part_deg, behind, (my_group + turn) % blocks, active
        )
        return (part_sum, part_deg, ahead_block, behind)

    totals, degree, _, _ = lax.fori_loop(
        1, half_cycle + 1, turn_double, (totals, degree, stale, stale)
    )
    summed, degrees = (
        lax.psum_scatter(
            totals.astype(jnp.bfloat16), "rep", scatter_dimension=0, tiled=True
        ).astype(jnp.float32),
        lax.psum_scatter(
            degree.astype(jnp.bfloat16), "rep", scatter_dimension=0, tiled=True
        ).astype(jnp.float32),
    )
    neighbour_mean = ((stale.astype(jnp.float32) + summed) / (1.0 + degrees)[:, None]).astype(
        jnp.bfloat16
    )
    hidden = jnp.dot(stale, w_self, preferred_element_type=jnp.float32) + jnp.dot(
        neighbour_mean, w_neigh, preferred_element_type=jnp.float32
    )
    active_out = jnp.maximum(hidden, 0.0)
    refreshed = active_out * lax.rsqrt(
        jnp.mean(active_out * active_out, axis=-1, keepdims=True) + 1e-05
    )
    return refreshed.astype(jnp.bfloat16)


def solution(mesh):
    return jax.shard_map(
        on_device,
        mesh=mesh,
        in_specs=(
            P(("blk", "rep"), None),
            P(),
            P(),
            P("blk", "rep", None, None, None, None),
            P("blk", "rep", None, None),
            P("blk", "rep", None),
        ),
        out_specs=P(("blk", "rep"), None),
        check_vma=False,
    )
```

profile of v0, /device:TPU:0, one launch (start us, length us, event | category | flops | bytes accessed | tf_op | source)
XLA Modules:
  0.0 93.5 jit_solution(9702987018728304456)
XLA Ops:
  6.5 0.7 copy-done.8
  7.8 0.6 compare_convert_fusion.2
  8.5 1.1 %convert_reduce_fusion.2 = f32[3,128]{1,0:T(4,128)S(1)} fusion(bf16[1,1,8,3,128,128]{5,4,3,2,1,0:T(8,128)(2,1)} %param.13, s32[]{:T(128)S(6)} %select_n.184, bf16[3]{0:T(256)(128)(2,1)S(1)} %compare_convert_fusion.2), kind=kLoop, calls=%fused_computation.35 | loop fusion | flops 147072 | bytes 99850 | tf_op jit(solution)/shard_map/reduce_sum | solution.py:43
  9.6 1.3 %fusion.13 = f32[3,128,512]{2,1,0:T(8,128)S(1)} fusion(bf16[128,512]{1,0:T(8,128)(2,1)} %param.10, bf16[1,1,8,3,128,128]{5,4,3,2,1,0:T(8,128)(2,1)} %param.13, s32[]{:T(128)S(6)} %select_n.184, bf16[3]{0:T(256)(128)(2,1)S(1)} %compare_convert_fusion.2), kind=kOutput, calls=%fused_computation.33 | convolution fusion | flops 50380800 | bytes 1015818 | tf_op jit(solution)/shard_map/kij,kjd->kid/dot_general | solution.py:36
  10.9 0.7 copy.19
  11.6 0.7 copy-done.10
  12.5 0.7 copy.10
  13.9 1.0 %scatter_fusion.4 = f32[4,128,512]{2,1,0:T(8,128)S(1)} fusion(f32[4,128,512]{2,1,0:T(8,128)S(1)} %reshape.248, s32[3]{0:T(128)S(1)} %fusion.20, f32[3,128,512]{2,1,0:T(8,128)S(1)} %fusion.13), kind=kCustom, calls=%fused_computation.4 | custom fusion | flops 196608 | bytes 2359308 | tf_op jit(solution)/shard_map/scatter-add | solution.py:40
  15.0 46.1 %while.22 = (s32[]{:T(128)}, f32[512,512]{1,0:T(8,128)S(1)}, f32[512]{0:T(512)S(1)}, bf16[128,512]{1,0:T(8,128)(2,1)}, bf16[128,512]{1,0:T(8,128)(2,1)S(1)}, /*i...) while((s32[]{:T(128)}, f32[512,512]{1,0:T(8,128)S(1)}, ...), condition=%wide.region_10.12_spmd, body=%wide.region_3.11_spmd.sunk | while | flops 101449792 | bytes 8533993 | solution.py:65
  15.5 2.9 %collective-permute-start.1 = (bf16[128,512]{1,0:T(8,128)(2,1)S(1)}, bf16[128,512]{1,0:T(8,128)(2,1)S(1)}, u32[]{:S(2)}, u32[]{:S(2)}) collective-permute-start(bf16[128,512]{1,0:T(8,128)(2,1)S(1)} %get-tuple-element.408), channel_id=1, source_target_pairs={{0,28},{4,0},{8,4},{12,8},{16,12},{20,16},{24,20},{28,24},{1,29},{... | collective-permute-start | bytes 393224 | tf_op jit(solution)/shard_map/while/body/eval_jaxpr/ppermute | solution.py:10
  18.4 0.7 fusion.36
  19.0 0.6 compare_convert_fusion.5
  19.7 0.8 fusion.35
  23.4 1.0 %scatter_fusion = f32[4,128,512]{2,1,0:T(8,128)S(1)} fusion(f32[4,128,512]{2,1,0:T(8,128)S(1)} %bitcast.77, s32[3]{0:T(128)S(1)} %get-tuple-element.384, f32[3,128,512]{2,1,0:T(8,128)S(1)} %fusion.37), kind=kCustom, calls=%fused_computation.clone.1 | custom fusion | flops 196608 | bytes 2359308 | tf_op jit(solution)/shard_map/while/body/eval_jaxpr/scatter-add | solution.py:40
  24.7 1.0 %scatter_fusion.1 = f32[4,128,512]{2,1,0:T(8,128)S(1)} fusion(f32[4,128,512]{2,1,0:T(8,128)S(1)} %scatter_fusion, s32[3]{0:T(128)S(1)} %get-tuple-element.386, f32[3,128,512]{2,1,0:T(8,128)S(1)} %fusion.38), kind=kCustom, calls=%fused_computation.1.clone.1 | custom fusion | flops 196608 | bytes 2359308 | tf_op jit(solution)/shard_map/while/body/eval_jaxpr/scatter-add | solution.py:40
  25.8 0.7 copy.29
  26.4 0.6 copy-done.9
  27.1 2.6 %collective-permute-start.1 = (bf16[128,512]{1,0:T(8,128)(2,1)S(1)}, bf16[128,512]{1,0:T(8,128)(2,1)S(1)}, u32[]{:S(2)}, u32[]{:S(2)}) collective-permute-start(bf16[128,512]{1,0:T(8,128)(2,1)S(1)} %get-tuple-element.408), channel_id=1, source_target_pairs={{0,28},{4,0},{8,4},{12,8},{16,12},{20,16},{24,20},{28,24},{1,29},{... | collective-permute-start | bytes 393224 | tf_op jit(solution)/shard_map/while/body/eval_jaxpr/ppermute | solution.py:10
  29.7 0.7 fusion.36
  30.4 0.6 compare_convert_fusion.5
  31.0 0.8 fusion.35
  33.2 0.6 scatter_fusion.2
  34.8 1.0 %scatter_fusion = f32[4,128,512]{2,1,0:T(8,128)S(1)} fusion(f32[4,128,512]{2,1,0:T(8,128)S(1)} %bitcast.77, s32[3]{0:T(128)S(1)} %get-tuple-element.384, f32[3,128,512]{2,1,0:T(8,128)S(1)} %fusion.37), kind=kCustom, calls=%fused_computation.clone.1 | custom fusion | flops 196608 | bytes 2359308 | tf_op jit(solution)/shard_map/while/body/eval_jaxpr/scatter-add | solution.py:40
  36.1 1.0 %scatter_fusion.1 = f32[4,128,512]{2,1,0:T(8,128)S(1)} fusion(f32[4,128,512]{2,1,0:T(8,128)S(1)} %scatter_fusion, s32[3]{0:T(128)S(1)} %get-tuple-element.386, f32[3,128,512]{2,1,0:T(8,128)S(1)} %fusion.38), kind=kCustom, calls=%fused_computation.1.clone.1 | custom fusion | flops 196608 | bytes 2359308 | tf_op jit(solution)/shard_map/while/body/eval_jaxpr/scatter-add | solution.py:40
  37.1 0.7 copy.29
  37.8 0.6 copy-done.9
  38.4 2.6 %collective-permute-start.1 = (bf16[128,512]{1,0:T(8,128)(2,1)S(1)}, bf16[128,512]{1,0:T(8,128)(2,1)S(1)}, u32[]{:S(2)}, u32[]{:S(2)}) collective-permute-start(bf16[128,512]{1,0:T(8,128)(2,1)S(1)} %get-tuple-element.408), channel_id=1, source_target_pairs={{0,28},{4,0},{8,4},{12,8},{16,12},{20,16},{24,20},{28,24},{1,29},{... | collective-permute-start | bytes 393224 | tf_op jit(solution)/shard_map/while/body/eval_jaxpr/ppermute | solution.py:10
  41.1 0.7 fusion.36
  41.7 0.6 compare_convert_fusion.5
  42.4 0.8 fusion.35
  46.1 1.0 %scatter_fusion = f32[4,128,512]{2,1,0:T(8,128)S(1)} fusion(f32[4,128,512]{2,1,0:T(8,128)S(1)} %bitcast.77, s32[3]{0:T(128)S(1)} %get-tuple-element.384, f32[3,128,512]{2,1,0:T(8,128)S(1)} %fusion.37), kind=kCustom, calls=%fused_computation.clone.1 | custom fusion | flops 196608 | bytes 2359308 | tf_op jit(solution)/shard_map/while/body/eval_jaxpr/scatter-add | solution.py:40
  47.4 1.0 %scatter_fusion.1 = f32[4,128,512]{2,1,0:T(8,128)S(1)} fusion(f32[4,128,512]{2,1,0:T(8,128)S(1)} %scatter_fusion, s32[3]{0:T(128)S(1)} %get-tuple-element.386, f32[3,128,512]{2,1,0:T(8,128)S(1)} %fusion.38), kind=kCustom, calls=%fused_computation.1.clone.1 | custom fusion | flops 196608 | bytes 2359308 | tf_op jit(solution)/shard_map/while/body/eval_jaxpr/scatter-add | solution.py:40
  48.4 0.7 copy.29
  49.1 0.6 copy-done.9
  49.8 2.6 %collective-permute-start.1 = (bf16[128,512]{1,0:T(8,128)(2,1)S(1)}, bf16[128,512]{1,0:T(8,128)(2,1)S(1)}, u32[]{:S(2)}, u32[]{:S(2)}) collective-permute-start(bf16[128,512]{1,0:T(8,128)(2,1)S(1)} %get-tuple-element.408), channel_id=1, source_target_pairs={{0,28},{4,0},{8,4},{12,8},{16,12},{20,16},{24,20},{28,24},{1,29},{... | collective-permute-start | bytes 393224 | tf_op jit(solution)/shard_map/while/body/eval_jaxpr/ppermute | solution.py:10
  52.4 0.7 fusion.36
  53.1 0.6 compare_convert_fusion.5
  53.7 0.8 fusion.35
  57.4 1.0 %scatter_fusion = f32[4,128,512]{2,1,0:T(8,128)S(1)} fusion(f32[4,128,512]{2,1,0:T(8,128)S(1)} %bitcast.77, s32[3]{0:T(128)S(1)} %get-tuple-element.384, f32[3,128,512]{2,1,0:T(8,128)S(1)} %fusion.37), kind=kCustom, calls=%fused_computation.clone.1 | custom fusion | flops 196608 | bytes 2359308 | tf_op jit(solution)/shard_map/while/body/eval_jaxpr/scatter-add | solution.py:40
  58.8 1.0 %scatter_fusion.1 = f32[4,128,512]{2,1,0:T(8,128)S(1)} fusion(f32[4,128,512]{2,1,0:T(8,128)S(1)} %scatter_fusion, s32[3]{0:T(128)S(1)} %get-tuple-element.386, f32[3,128,512]{2,1,0:T(8,128)S(1)} %fusion.38), kind=kCustom, calls=%fused_computation.1.clone.1 | custom fusion | flops 196608 | bytes 2359308 | tf_op jit(solution)/shard_map/while/body/eval_jaxpr/scatter-add | solution.py:40
  59.8 0.7 copy.29
  60.5 0.6 copy-done.9
  61.1 0.9 convert_element_type.86
  62.0 0.6 copy-done.11
  63.9 13.0 %all-reduce = bf16[512]{0:T(512)(128)(2,1)S(1)} all-reduce(bf16[512]{0:T(512)(128)(2,1)S(1)} %convert_element_type.88), channel_id=3, replica_groups=mesh['blk'=8,'rep'=4] {'rep'}, use_global_device_ids=true, to_apply=%region_12.14.clone | all-reduce | flops 512 | bytes 2048
  77.3 7.4 %reduce-scatter.2.cloned.1.call-done = bf16[128,512]{1,0:T(8,128)(2,1)} async-done(((bf16[512,512]{1,0:T(8,128)(2,1)}), bf16[128,512]{1,0:T(8,128)(2,1)}) %reduce-scatter.2.cloned.1.call-update) | async-done | bytes 131088 | tf_op jit(solution)/shard_map/reduce_scatter | solution.py:69
  84.7 1.3 %multiply_reduce_fusion = (f32[128]{0:T(128)S(1)}, f32[128,512]{1,0:T(8,128)S(1)}) fusion(f32[128,512]{1,0:T(8,128)S(1)} %fusion.23, bf16[512,512]{1,0:T(8,128)(2,1)S(1)} %copy-done, bf16[128,512]{1,0:T(8,128)(2,1)} %reduce-scatter.2.cloned.1.call-done, bf16[128,512]{1,0:T(8,128)(2,1)S(1)} %copy-done.3, f32[128]{0:T(128)S(1)} %fusion.21), kind=kOutput, calls=%fused_computation.31 | convolution fusion | flops 67698560 | bytes 1311744 | tf_op jit(solution)/shard_map/dot_general | solution.py:79
  85.9 0.8 multiply_convert_fusion
  (86 shorter events, 12.8 us)
Async XLA Ops:
  6.5 78.1 %copy-start = (bf16[512,512]{1,0:T(8,128)(2,1)S(1)}, bf16[512,512]{1,0:T(8,128)(2,1)}, u32[]{:S(2)}) copy-start(bf16[512,512]{1,0:T(8,128)(2,1)} %param.12) | copy-start | bytes 1572868
  6.5 78.1 %reduce-scatter.2.cloned.1.call-start = ((), (), s32[]{:S(2)}) async-start(), calls=%async_computation.1 | async-start | bytes 655360 | tf_op jit(solution)/shard_map/reduce_scatter | solution.py:69
  6.5 0.7 copy-start.8
  9.6 1.3 %copy-start.2 = (bf16[128,512]{1,0:T(8,128)(2,1)S(1)}, bf16[128,512]{1,0:T(8,128)(2,1)}, u32[]{:S(2)}) copy-start(bf16[128,512]{1,0:T(8,128)(2,1)} %param.10) | copy-start | bytes 393220
  11.6 0.7 copy-start.10
  13.9 1.1 %copy-start.1 = (bf16[1,1,8,3,128,128]{5,4,3,2,1,0:T(8,128)(2,1)S(1)}, bf16[1,1,8,3,128,128]{5,4,3,2,1,0:T(8,128)(2,1)}, u32[]{:S(2)}) copy-start(bf16[1,1,8,3,128,128]{5,4,3,2,1,0:T(8,128)(2,1)} %param.13) | copy-start | bytes 2359300
  13.9 1.1 %copy-start.4 = (bf16[128,512]{1,0:T(8,128)(2,1)S(1)}, bf16[128,512]{1,0:T(8,128)(2,1)}, u32[]{:S(2)}) copy-start(bf16[128,512]{1,0:T(8,128)(2,1)} %param.10) | copy-start | bytes 393220
  15.0 8.1 %collective-permute-start = (bf16[128,512]{1,0:T(8,128)(2,1)}, bf16[128,512]{1,0:T(8,128)(2,1)S(1)}, u32[]{:S(2)}, u32[]{:S(2)}) collective-permute-start(bf16[128,512]{1,0:T(8,128)(2,1)} %get-tuple-element.407), channel_id=1, source_target_pairs={{0,4},{4,8},{8,12},{12,16},{16,20},{20,24},{24,28},{28,0},{1,5},{5... | collective-permute-start | bytes 393224 | tf_op jit(solution)/shard_map/while/body/eval_jaxpr/ppermute | solution.py:10
  15.5 8.9 %collective-permute-start.1 = (bf16[128,512]{1,0:T(8,128)(2,1)S(1)}, bf16[128,512]{1,0:T(8,128)(2,1)S(1)}, u32[]{:S(2)}, u32[]{:S(2)}) collective-permute-start(bf16[128,512]{1,0:T(8,128)(2,1)S(1)} %get-tuple-element.408), channel_id=1, source_target_pairs={{0,28},{4,0},{8,4},{12,8},{16,12},{20,16},{24,20},{28,24},{1,29},{... | collective-permute-start | bytes 393224 | tf_op jit(solution)/shard_map/while/body/eval_jaxpr/ppermute | solution.py:10
  21.1 0.5 copy-start.6
  23.4 1.0 %copy-start.7 = (bf16[3]{0:T(256)(128)(2,1)S(1)}, bf16[3]{0:T(256)(128)(2,1)}, u32[]{:S(2)}) copy-start(bf16[3]{0:T(256)(128)(2,1)} %copy-done.6) | copy-start | bytes 22 | tf_op jit(solution)/shard_map/while
  26.4 0.7 copy-start.9
  27.1 7.3 %collective-permute-start = (bf16[128,512]{1,0:T(8,128)(2,1)}, bf16[128,512]{1,0:T(8,128)(2,1)S(1)}, u32[]{:S(2)}, u32[]{:S(2)}) collective-permute-start(bf16[128,512]{1,0:T(8,128)(2,1)} %get-tuple-element.407), channel_id=1, source_target_pairs={{0,4},{4,8},{8,12},{12,16},{16,20},{20,24},{24,28},{28,0},{1,5},{5... | collective-permute-start | bytes 393224 | tf_op jit(solution)/shard_map/while/body/eval_jaxpr/ppermute | solution.py:10
  27.1 8.7 %collective-permute-start.1 = (bf16[128,512]{1,0:T(8,128)(2,1)S(1)}, bf16[128,512]{1,0:T(8,128)(2,1)S(1)}, u32[]{:S(2)}, u32[]{:S(2)}) collective-permute-start(bf16[128,512]{1,0:T(8,128)(2,1)S(1)} %get-tuple-element.408), channel_id=1, source_target_pairs={{0,28},{4,0},{8,4},{12,8},{16,12},{20,16},{24,20},{28,24},{1,29},{... | collective-permute-start | bytes 393224 | tf_op jit(solution)/shard_map/while/body/eval_jaxpr/ppermute | solution.py:10
  32.4 0.5 copy-start.6
  34.7 1.0 %copy-start.7 = (bf16[3]{0:T(256)(128)(2,1)S(1)}, bf16[3]{0:T(256)(128)(2,1)}, u32[]{:S(2)}) copy-start(bf16[3]{0:T(256)(128)(2,1)} %copy-done.6) | copy-start | bytes 22 | tf_op jit(solution)/shard_map/while
  37.8 0.7 copy-start.9
  38.4 7.3 %collective-permute-start = (bf16[128,512]{1,0:T(8,128)(2,1)}, bf16[128,512]{1,0:T(8,128)(2,1)S(1)}, u32[]{:S(2)}, u32[]{:S(2)}) collective-permute-start(bf16[128,512]{1,0:T(8,128)(2,1)} %get-tuple-element.407), channel_id=1, source_target_pairs={{0,4},{4,8},{8,12},{12,16},{16,20},{20,24},{24,28},{28,0},{1,5},{5... | collective-permute-start | bytes 393224 | tf_op jit(solution)/shard_map/while/body/eval_jaxpr/ppermute | solution.py:10
  38.4 8.7 %collective-permute-start.1 = (bf16[128,512]{1,0:T(8,128)(2,1)S(1)}, bf16[128,512]{1,0:T(8,128)(2,1)S(1)}, u32[]{:S(2)}, u32[]{:S(2)}) collective-permute-start(bf16[128,512]{1,0:T(8,128)(2,1)S(1)} %get-tuple-element.408), channel_id=1, source_target_pairs={{0,28},{4,0},{8,4},{12,8},{16,12},{20,16},{24,20},{28,24},{1,29},{... | collective-permute-start | bytes 393224 | tf_op jit(solution)/shard_map/while/body/eval_jaxpr/ppermute | solution.py:10
  43.8 0.5 copy-start.6
  46.1 1.0 %copy-start.7 = (bf16[3]{0:T(256)(128)(2,1)S(1)}, bf16[3]{0:T(256)(128)(2,1)}, u32[]{:S(2)}) copy-start(bf16[3]{0:T(256)(128)(2,1)} %copy-done.6) | copy-start | bytes 22 | tf_op jit(solution)/shard_map/while
  49.1 0.7 copy-start.9
  49.8 7.3 %collective-permute-start = (bf16[128,512]{1,0:T(8,128)(2,1)}, bf16[128,512]{1,0:T(8,128)(2,1)S(1)}, u32[]{:S(2)}, u32[]{:S(2)}) collective-permute-start(bf16[128,512]{1,0:T(8,128)(2,1)} %get-tuple-element.407), channel_id=1, source_target_pairs={{0,4},{4,8},{8,12},{12,16},{16,20},{20,24},{24,28},{28,0},{1,5},{5... | collective-permute-start | bytes 393224 | tf_op jit(solution)/shard_map/while/body/eval_jaxpr/ppermute | solution.py:10
  49.8 8.7 %collective-permute-start.1 = (bf16[128,512]{1,0:T(8,128)(2,1)S(1)}, bf16[128,512]{1,0:T(8,128)(2,1)S(1)}, u32[]{:S(2)}, u32[]{:S(2)}) collective-permute-start(bf16[128,512]{1,0:T(8,128)(2,1)S(1)} %get-tuple-element.408), channel_id=1, source_target_pairs={{0,28},{4,0},{8,4},{12,8},{16,12},{20,16},{24,20},{28,24},{1,29},{... | collective-permute-start | bytes 393224 | tf_op jit(solution)/shard_map/while/body/eval_jaxpr/ppermute | solution.py:10
  55.1 0.5 copy-start.6
  57.4 1.0 %copy-start.7 = (bf16[3]{0:T(256)(128)(2,1)S(1)}, bf16[3]{0:T(256)(128)(2,1)}, u32[]{:S(2)}) copy-start(bf16[3]{0:T(256)(128)(2,1)} %copy-done.6) | copy-start | bytes 22 | tf_op jit(solution)/shard_map/while
  60.5 0.7 copy-start.9
  61.1 15.9 %copy-start.5 = (bf16[512,512]{1,0:T(8,128)(2,1)S(1)}, bf16[512,512]{1,0:T(8,128)(2,1)}, u32[]{:S(2)}) copy-start(bf16[512,512]{1,0:T(8,128)(2,1)} %param.11) | copy-start | bytes 1572868
  62.0 15.1 %copy-start.3 = (bf16[128,512]{1,0:T(8,128)(2,1)S(1)}, bf16[128,512]{1,0:T(8,128)(2,1)}, u32[]{:S(2)}) copy-start(bf16[128,512]{1,0:T(8,128)(2,1)} %param.10) | copy-start | bytes 393220
  62.0 0.7 copy-start.11
Sparse Core Ops, SparseCore 0:
  62.1 22.5 reduce-scatter.1
where the time goes:
time: 94.1 us; the launch traced here: 93.5 us
  other arithmetic  24.4 us (26%)
  local copies, waits for them, and re-layouts  15 us (16%)
  between operations  14.2 us (15%)
  blocking collectives  13 us (14%)
  starting transfers between devices  11.3 us (12%)
  waiting for transfers between devices  7.44 us (8%)
  matrix products  5.16 us (5%)
  loops' own time  3.03 us (3%)
    unnamed x1, blocking collectives  13 us
    ppermute x8, starting transfers between devices, passed_along(): return lax.ppermute(value, axis, pairs)  11.3 us
    scatter-add x9, other arithmetic, take_tiles(): totals = totals.reshape(row_tiles, tile_size, width).at[row_tile].add(pro...  9 us
    while x32, local copies, waits for them, and re-layouts  7.41 us
    reduce_scatter x1, waiting for transfers between devices, on_device(): lax.psum_scatter(totals.astype(jnp.bfloat16), 'rep', scatter_dimension=0,...  7.4 us
    scatter-add x9, other arithmetic, take_tiles(): degree.reshape(row_tiles, tile_size).at[row_tile].add(row_sums)  5.26 us
    dot_general x9, matrix products, take_tiles(): jnp.einsum('kij,kjd->kid', tiles, picked, preferred_element_type=jnp.floa...  3.68 us
    unnamed x20, local copies, waits for them, and re-layouts  3.42 us
  transfers between devices with their start and end apart: 9, of which 1 were waited for; matrix products, arithmetic and copies ran while one was open for 21% of the time, Pallas kernels for 0%

commit v1 on v0

v1 whole, which is shorter than its diff:
```python
import functools

import jax
import jax.numpy as jnp
from jax import lax
from jax.experimental import pallas as pl
from jax.experimental.pallas import tpu as pltpu
from jax.sharding import PartitionSpec as P

MESH = pl.DeviceIdType.MESH
CHUNKS = 4


def refresh_kernel(
    blocks, members, stale_ref, w_self_hbm, w_neigh_hbm, weights_hbm, places_ref, counts_ref,
    out_ref,
    w_self, w_neigh, weights, adjacency, gathered, partial, arrived, deg_send, deg_recv, total,
    load_sem, g_send, g_recv, f_send, f_recv, p_send, p_recv, d_send, d_recv,
):
    own, width = stale_ref.shape
    cap, tile = weights_hbm.shape[3], weights_hbm.shape[4]
    col_tiles = own // tile
    chips = blocks // 2
    chunk = width // CHUNKS
    my_blk = lax.axis_index("blk")
    my_rep = lax.axis_index("rep")
    chip, core = my_blk // 2, my_blk % 2

    def load(slot, source, target):
        return pltpu.make_async_copy(source, target, load_sem.at[slot])

    loads = [
        load(0, weights_hbm.at[0, 0], weights.at[pl.ds(0, blocks)]),
        load(1, w_self_hbm, w_self),
        load(2, w_neigh_hbm, w_neigh),
    ]
    for copy in loads:
        copy.start()

    pair = {"blk": chip * 2 + 1 - core}
    def chip_at(offset):
        return {"blk": ((chip + offset) % chips) * 2 + core}
    def member_at(offset):
        return {"rep": (my_rep + offset) % members}

    barrier = pltpu.get_barrier_semaphore()
    peers = [member_at(d) for d in range(1, members)]
    peers += [chip_at(o) for o in range(1, chips)] + [pair]
    for peer in peers:
        pl.semaphore_signal(barrier, inc=1, device_id=peer, device_id_type=MESH)

    def columns(h):
        return pl.ds(h * chunk, chunk)

    def to_chip(h, o):
        return pltpu.make_async_remote_copy(
            src_ref=stale_ref.at[:, columns(h)], dst_ref=gathered.at[h, 2 * o],
            send_sem=g_send.at[h, o], recv_sem=g_recv.at[h, o],
            device_id=chip_at(o), device_id_type=MESH)

    def to_pair(h, o):
        source = stale_ref.at[:, columns(h)] if o == 0 else gathered.at[h, 2 * o]
        return pltpu.make_async_remote_copy(
            src_ref=source, dst_ref=gathered.at[h, 2 * o + 1],
            send_sem=f_send.at[h, o], recv_sem=f_recv.at[h, o],
            device_id=pair, device_id_type=MESH)

    def to_member(h, d):
        return pltpu.make_async_remote_copy(
            src_ref=partial.at[h, d], dst_ref=arrived.at[h, d - 1],
            send_sem=p_send.at[h, d - 1], recv_sem=p_recv.at[h, d - 1],
            device_id=member_at(d), device_id_type=MESH)

    def degree_to(d):
        return pltpu.make_async_remote_copy(
            src_ref=deg_send.at[d], dst_ref=deg_recv.at[d - 1],
            send_sem=d_send.at[d - 1], recv_sem=d_recv.at[d - 1],
            device_id=member_at(d), device_id_type=MESH)

    pl.semaphore_wait(barrier, len(peers))
    for h in range(CHUNKS):
        for o in range(1, chips):
            to_chip(h, o).start()
        to_pair(h, 0).start()

    for h in range(CHUNKS):
        gathered[h, 0] = stale_ref[:, h * chunk:(h + 1) * chunk]
    weights[blocks] = jnp.zeros_like(weights[blocks])

    loads[0].wait()
    def place_tiles(slot):
        source = ((chip + chips - slot // 2) % chips) * 2 + (core + slot % 2) % 2
        live = counts_ref[0, 0, source]
        spots = [
            jnp.where(k < live, places_ref[0, k, 0, source], -1) for k in range(cap)
        ]
        for q in range(members * col_tiles):
            row = ((my_rep + q // col_tiles) % members) * col_tiles + q % col_tiles
            for column in range(col_tiles):
                spot = row * col_tiles + column
                block, index = jnp.int32(blocks), jnp.int32(0)
                for k in range(cap):
                    hit = spots[k] == spot
                    block = jnp.where(hit, source, block)
                    index = jnp.where(hit, k, index)
                start = slot * own + column * tile
                if not isinstance(slot, int):
                    start = pl.multiple_of(start, tile)
                adjacency[q * tile:(q + 1) * tile, pl.ds(start, tile)] = weights[block, index]

    if blocks <= 8:
        for slot in range(blocks):
            place_tiles(slot)
    else:
        @pl.loop(0, blocks)
        def _(slot):
            place_tiles(slot)

    ones = jnp.ones((16, blocks * own), jnp.bfloat16)
    for d in range(members):
        deg_send[d] = lax.dot_general(
            ones, adjacency[d * own:(d + 1) * own, :], (((1,), (1,)), ((), ())),
            preferred_element_type=jnp.float32).astype(jnp.bfloat16)
    for d in range(1, members):
        degree_to(d).start()

    group = min(members, max(1, 512 // own))
    for h in range(CHUNKS):
        for o in range(1, chips):
            to_chip(h, o).wait_recv()
            to_pair(h, o).start()
        for o in range(chips):
            to_pair(h, o).wait_recv()
        sources = gathered[h].reshape(blocks * own, chunk)
        for first in range(0, members, group):
            last = min(first + group, members)
            sums = jnp.dot(adjacency[first * own:last * own, :], sources,
                           preferred_element_type=jnp.float32).astype(jnp.bfloat16)
            partial[h, first:last] = sums.reshape(last - first, own, chunk)
            for d in range(max(first, 1), last):
                to_member(h, d).start()

    loads[1].wait()
    total[...] = jnp.dot(stale_ref[...], w_self[...], preferred_element_type=jnp.float32)
    degree = deg_send[0].astype(jnp.float32)
    for d in range(1, members):
        degree_to(d).wait_recv()
        degree = degree + deg_recv[d - 1].astype(jnp.float32)
    inverse = jnp.transpose(jnp.broadcast_to(1.0 / (1.0 + degree[0:1]), (own, own)))[:, 0:1]
    loads[2].wait()
    for h in range(CHUNKS):
        summed = partial[h, 0].astype(jnp.float32)
        for d in range(1, members):
            to_member(h, d).wait_recv()
            summed = summed + arrived[h, d - 1].astype(jnp.float32)
        own_rows = stale_ref[:, h * chunk:(h + 1) * chunk].astype(jnp.float32)
        mean = ((own_rows + summed) * inverse).astype(jnp.bfloat16)
        total[...] += jnp.dot(mean, w_neigh[h * chunk:(h + 1) * chunk, :],
                              preferred_element_type=jnp.float32)
    active = jnp.maximum(total[...], 0.0)
    scale = lax.rsqrt(jnp.mean(active * active, axis=-1, keepdims=True) + 1e-05)
    out_ref[...] = (active * scale).astype(out_ref.dtype)

    for h in range(CHUNKS):
        for o in range(1, chips):
            to_chip(h, o).wait_send()
        for o in range(chips):
            to_pair(h, o).wait_send()
        for d in range(1, members):
            to_member(h, d).wait_send()
    for d in range(1, members):
        degree_to(d).wait_send()


def on_device(stale, w_self, w_neigh, tile_weights, tile_pos, tile_counts):
    blocks = lax.axis_size("blk")
    members = lax.axis_size("rep")
    own, width = stale.shape
    cap, tile = tile_weights.shape[3], tile_weights.shape[4]
    chips = blocks // 2
    chunk = width // CHUNKS
    bf16, f32 = jnp.bfloat16, jnp.float32
    dma = pltpu.SemaphoreType.DMA
    vmem = pl.BlockSpec(memory_space=pltpu.VMEM)
    smem = pl.BlockSpec(memory_space=pltpu.SMEM)
    hbm = pl.BlockSpec(memory_space=pl.ANY)
    flops = 2 * own * width * (members * own * blocks + 2 * width)
    return pl.pallas_call(
        functools.partial(refresh_kernel, blocks, members),
        out_shape=jax.ShapeDtypeStruct((own, width), bf16),
        in_specs=[vmem, hbm, hbm, hbm, smem, smem],
        out_specs=vmem,
        scratch_shapes=[
            pltpu.VMEM(w_self.shape, bf16),
            pltpu.VMEM(w_neigh.shape, bf16),
            pltpu.VMEM((blocks + 1, cap, tile, tile), bf16),
            pltpu.VMEM((members * own, blocks * own), bf16),
            pltpu.VMEM((CHUNKS, blocks, own, chunk), bf16),
            pltpu.VMEM((CHUNKS, members, own, chunk), bf16),
            pltpu.VMEM((CHUNKS, members - 1, own, chunk), bf16),
            pltpu.VMEM((members, 16, own), bf16),
            pltpu.VMEM((members - 1, 16, own), bf16),
            pltpu.VMEM((own, width), f32),
            dma((3,)),
            dma((CHUNKS, chips)),
            dma((CHUNKS, chips)),
            dma((CHUNKS, chips)),
            dma((CHUNKS, chips)),
            dma((CHUNKS, members - 1)),
            dma((CHUNKS, members - 1)),
            dma((members - 1,)),
            dma((members - 1,)),
        ],
        compiler_params=pltpu.CompilerParams(
            collective_id=0, has_side_effects=True, vmem_limit_bytes=60 * 1024 * 1024),
        cost_estimate=pl.CostEstimate(
            flops=flops, bytes_accessed=2 * (tile_weights.size + 4 * own * width), transcendentals=own),
        name="refresh",
    )(stale, w_self, w_neigh, tile_weights, jnp.transpose(tile_pos, (0, 3, 1, 2)), tile_counts)


def solution(mesh):
    return jax.shard_map(
        on_device,
        mesh=mesh,
        in_specs=(
            P(("blk", "rep"), None),
            P(),
            P(),
            P("blk", "rep", None, None, None, None),
            P("blk", "rep", None, None),
            P("blk", "rep", None),
        ),
        out_specs=P(("blk", "rep"), None),
        check_vma=False,
    )
```

time: 94.1 us -> 27.7 us (0.29)
  Pallas kernels: 0 us -> 26 us
  other arithmetic: 24.4 us -> 0 us
  between operations: 14.2 us -> 0.01 us
  local copies, waits for them, and re-layouts: 15 us -> 1.57 us
  blocking collectives: 13 us -> 0 us
  starting transfers between devices: 11.3 us -> 0 us
  waiting for transfers between devices: 7.44 us -> 0 us
  matrix products: 5.16 us -> 0 us
  loops' own time: 3.03 us -> 0 us
    pallas_call x0 -> x1, Pallas kernels: none -> 26 us  [on_device(): pl.pallas_call(functools.partial(refresh_kernel, blocks, members), out_sh...]
    scatter-add x18 -> x0, other arithmetic: 14.3 us -> none  [the longest x9 9 us: take_tiles(): totals = totals.reshape(row_tiles, tile_size, width).at[row_tile].add(pro...]
    unnamed x1 -> x0, blocking collectives: 13 us -> none
    ppermute x8 -> x0, starting transfers between devices: 11.3 us -> none  [passed_along(): return lax.ppermute(value, axis, pairs)]
    while x33 -> x0, local copies, waits for them, and re-layouts: 8.09 us -> none
    reduce_scatter x1 -> x0, waiting for transfers between devices: 7.4 us -> none  [on_device(): lax.psum_scatter(totals.astype(jnp.bfloat16), 'rep', scatter_dimension=0,...]
    dot_general x11 -> x0, matrix products: 5.16 us -> none  [the longest x9 3.68 us: take_tiles(): jnp.einsum('kij,kjd->kid', tiles, picked, preferred_element_type=jnp.floa...]
    convert_element_type x12 -> x0, other arithmetic: 4.81 us -> none  [the longest x9 3.2 us: take_tiles(): live_mask = (jnp.arange(capacity) < live_count).astype(jnp.bfloat16)]
  transfers between devices with their start and end apart: 9 -> 0, of which waited for: 1 -> 0; matrix products, arithmetic and copies ran while one was open for 21% -> 0% of each run, Pallas kernels for 0% -> 0%
where the time goes in v1:
time: 27.7 us; the launch traced here: 27.6 us
  Pallas kernels  26 us (94%)
  local copies, waits for them, and re-layouts  1.57 us (6%)
    pallas_call x1, Pallas kernels, on_device(): pl.pallas_call(functools.partial(refresh_kernel, blocks, members), out_sh...  26 us
    unnamed x1, local copies, waits for them, and re-layouts  1.57 us

profile of v1, /device:TPU:0, one launch (start us, length us, event | category | flops | bytes accessed | tf_op | source)
XLA Modules:
  0.0 27.6 jit_solution(4418785888915250152)
XLA Ops:
  0.0 26.0 %refresh.1 = bf16[128,512]{1,0:T(8,128)(2,1)} custom-call(bf16[128,512]{1,0:T(8,128)(2,1)} %stale_ref.1, bf16[512,512]{1,0:T(8,128)(2,1)} %w_self_hbm.1, bf16[512,512]{1,0:T(8,128)(2,1)} %w_neigh_hbm.1, bf16[1,1,8,3,128,128]{5,4,3,2,1,0:T(8,128)(2,1)} %weights_hbm.1, s32[1,3,1,8]{3,2,1,0:T(1,128)} %bitcast.1, s32[1,1,8]{2,1,0:T(1,128)} %counts_ref.1), custom_call_target="tpu_custom_call" | custom-call | flops 671088640 | bytes 1310720 | tf_op jit(solution)/shard_map/refresh/pallas_call | solution.py:188
  26.0 1.6 %copy.8 = bf16[128,512]{1,0:T(8,128)(2,1)} copy(bf16[128,512]{1,0:T(8,128)(2,1)} %refresh.1) | data formatting | bytes 262144

commit v2 on v1

--- a/solution.py
+++ b/solution.py
@@ -12,12 +12,12 @@
 
 
 def refresh_kernel(
-    blocks, members, stale_ref, w_self_hbm, w_neigh_hbm, weights_hbm, places_ref, counts_ref,
+    blocks, members, stale_hbm, w_self_hbm, w_neigh_hbm, weights_hbm, places_hbm, counts_hbm,
     out_ref,
-    w_self, w_neigh, weights, adjacency, gathered, partial, arrived, deg_send, deg_recv, total,
+    places_ref, counts_ref, w_self, w_neigh, weights, adjacency, gathered, partial, arrived, deg_send, deg_recv, total,
     load_sem, g_send, g_recv, f_send, f_recv, p_send, p_recv, d_send, d_recv,
 ):
-    own, width = stale_ref.shape
+    own, width = stale_hbm.shape
     cap, tile = weights_hbm.shape[3], weights_hbm.shape[4]
     col_tiles = own // tile
     chips = blocks // 2
@@ -29,13 +29,15 @@
     def load(slot, source, target):
         return pltpu.make_async_copy(source, target, load_sem.at[slot])
 
-    loads = [
-        load(0, weights_hbm.at[0, 0], weights.at[pl.ds(0, blocks)]),
-        load(1, w_self_hbm, w_self),
-        load(2, w_neigh_hbm, w_neigh),
+    own_loads = [
+        load(h, stale_hbm.at[:, pl.ds(h * chunk, chunk)], gathered.at[h, 0])
+        for h in range(CHUNKS)
     ]
-    for copy in loads:
-        copy.start()
+    place_load = load(CHUNKS, places_hbm, places_ref)
+    count_load = load(CHUNKS + 1, counts_hbm, counts_ref)
+    tile_load = load(CHUNKS + 2, weights_hbm.at[0, 0], weights.at[pl.ds(0, blocks)])
+    self_load = load(CHUNKS + 3, w_self_hbm, w_self)
+    neigh_load = load(CHUNKS + 4, w_neigh_hbm, w_neigh)
 
     pair = {"blk": chip * 2 + 1 - core}
     def chip_at(offset):
@@ -48,20 +50,18 @@
     peers += [chip_at(o) for o in range(1, chips)] + [pair]
     for peer in peers:
         pl.semaphore_signal(barrier, inc=1, device_id=peer, device_id_type=MESH)
-
-    def columns(h):
-        return pl.ds(h * chunk, chunk)
+    for copy in own_loads + [place_load, count_load, tile_load, self_load, neigh_load]:
+        copy.start()
 
     def to_chip(h, o):
         return pltpu.make_async_remote_copy(
-            src_ref=stale_ref.at[:, columns(h)], dst_ref=gathered.at[h, 2 * o],
+            src_ref=gathered.at[h, 0], dst_ref=gathered.at[h, 2 * o],
             send_sem=g_send.at[h, o], recv_sem=g_recv.at[h, o],
             device_id=chip_at(o), device_id_type=MESH)
 
     def to_pair(h, o):
-        source = stale_ref.at[:, columns(h)] if o == 0 else gathered.at[h, 2 * o]
-        return pltpu.make_async_remote_copy(
-            src_ref=source, dst_ref=gathered.at[h, 2 * o + 1],
+        return pltpu.make_async_remote_copy(
+            src_ref=gathered.at[h, 2 * o], dst_ref=gathered.at[h, 2 * o + 1],
             send_sem=f_send.at[h, o], recv_sem=f_recv.at[h, o],
             device_id=pair, device_id_type=MESH)
 
@@ -77,17 +77,19 @@
             send_sem=d_send.at[d - 1], recv_sem=d_recv.at[d - 1],
             device_id=member_at(d), device_id_type=MESH)
 
+    for copy in own_loads:
+        copy.wait()
     pl.semaphore_wait(barrier, len(peers))
     for h in range(CHUNKS):
         for o in range(1, chips):
             to_chip(h, o).start()
         to_pair(h, 0).start()
 
-    for h in range(CHUNKS):
-        gathered[h, 0] = stale_ref[:, h * chunk:(h + 1) * chunk]
     weights[blocks] = jnp.zeros_like(weights[blocks])
 
-    loads[0].wait()
+    place_load.wait()
+    count_load.wait()
+    tile_load.wait()
     def place_tiles(slot):
         source = ((chip + chips - slot // 2) % chips) * 2 + (core + slot % 2) % 2
         live = counts_ref[0, 0, source]
@@ -116,14 +118,6 @@
         def _(slot):
             place_tiles(slot)
 
-    ones = jnp.ones((16, blocks * own), jnp.bfloat16)
-    for d in range(members):
-        deg_send[d] = lax.dot_general(
-            ones, adjacency[d * own:(d + 1) * own, :], (((1,), (1,)), ((), ())),
-            preferred_element_type=jnp.float32).astype(jnp.bfloat16)
-    for d in range(1, members):
-        degree_to(d).start()
-
     group = min(members, max(1, 512 // own))
     for h in range(CHUNKS):
         for o in range(1, chips):
@@ -139,21 +133,32 @@
             partial[h, first:last] = sums.reshape(last - first, own, chunk)
             for d in range(max(first, 1), last):
                 to_member(h, d).start()
-
-    loads[1].wait()
-    total[...] = jnp.dot(stale_ref[...], w_self[...], preferred_element_type=jnp.float32)
+        if h == 0:
+            ones = jnp.ones((16, blocks * own), jnp.bfloat16)
+            for d in range(members):
+                deg_send[d] = lax.dot_general(
+                    ones, adjacency[d * own:(d + 1) * own, :], (((1,), (1,)), ((), ())),
+                    preferred_element_type=jnp.float32).astype(jnp.bfloat16)
+            for d in range(1, members):
+                degree_to(d).start()
+
+    self_load.wait()
+    total[...] = jnp.dot(gathered[0, 0], w_self[0:chunk, :], preferred_element_type=jnp.float32)
+    for h in range(1, CHUNKS):
+        total[...] += jnp.dot(gathered[h, 0], w_self[h * chunk:(h + 1) * chunk, :],
+                              preferred_element_type=jnp.float32)
     degree = deg_send[0].astype(jnp.float32)
     for d in range(1, members):
         degree_to(d).wait_recv()
         degree = degree + deg_recv[d - 1].astype(jnp.float32)
     inverse = jnp.transpose(jnp.broadcast_to(1.0 / (1.0 + degree[0:1]), (own, own)))[:, 0:1]
-    loads[2].wait()
+    neigh_load.wait()
     for h in range(CHUNKS):
         summed = partial[h, 0].astype(jnp.float32)
         for d in range(1, members):
             to_member(h, d).wait_recv()
             summed = summed + arrived[h, d - 1].astype(jnp.float32)
-        own_rows = stale_ref[:, h * chunk:(h + 1) * chunk].astype(jnp.float32)
+        own_rows = gathered[h, 0].astype(jnp.float32)
         mean = ((own_rows + summed) * inverse).astype(jnp.bfloat16)
         total[...] += jnp.dot(mean, w_neigh[h * chunk:(h + 1) * chunk, :],
                               preferred_element_type=jnp.float32)
@@ -182,15 +187,16 @@
     bf16, f32 = jnp.bfloat16, jnp.float32
     dma = pltpu.SemaphoreType.DMA
     vmem = pl.BlockSpec(memory_space=pltpu.VMEM)
-    smem = pl.BlockSpec(memory_space=pltpu.SMEM)
     hbm = pl.BlockSpec(memory_space=pl.ANY)
     flops = 2 * own * width * (members * own * blocks + 2 * width)
     return pl.pallas_call(
         functools.partial(refresh_kernel, blocks, members),
         out_shape=jax.ShapeDtypeStruct((own, width), bf16),
-        in_specs=[vmem, hbm, hbm, hbm, smem, smem],
+        in_specs=[hbm] * 6,
         out_specs=vmem,
         scratch_shapes=[
+            pltpu.SMEM((1, cap, 1, blocks), jnp.int32),
+            pltpu.SMEM((1, 1, blocks), jnp.int32),
             pltpu.VMEM(w_self.shape, bf16),
             pltpu.VMEM(w_neigh.shape, bf16),
             pltpu.VMEM((blocks + 1, cap, tile, tile), bf16),
@@ -201,7 +207,7 @@
             pltpu.VMEM((members, 16, own), bf16),
             pltpu.VMEM((members - 1, 16, own), bf16),
             pltpu.VMEM((own, width), f32),
-            dma((3,)),
+            dma((CHUNKS + 5,)),
             dma((CHUNKS, chips)),
             dma((CHUNKS, chips)),
             dma((CHUNKS, chips)),

time: 27.7 us -> 27.1 us (0.978)
  Pallas kernels: 26 us -> 25.4 us
    pallas_call x1, Pallas kernels: 26 us -> 25.4 us  [on_device(): pl.pallas_call(functools.partial(refresh_kernel, blocks, members), out_sh...]
where the time goes in v2:
time: 27.1 us; the launch traced here: 27 us
  Pallas kernels  25.4 us (94%)
  local copies, waits for them, and re-layouts  1.57 us (6%)
    pallas_call x1, Pallas kernels, on_device(): pl.pallas_call(functools.partial(refresh_kernel, blocks, members), out_sh...  25.4 us
    unnamed x1, local copies, waits for them, and re-layouts  1.57 us

profile of v2, /device:TPU:0, one launch (start us, length us, event | category | flops | bytes accessed | tf_op | source)
XLA Modules:
  0.0 27.0 jit_solution(7684785615862708519)
XLA Ops:
  0.0 25.4 %refresh.1 = bf16[128,512]{1,0:T(8,128)(2,1)} custom-call(bf16[128,512]{1,0:T(8,128)(2,1)} %stale_hbm.1, bf16[512,512]{1,0:T(8,128)(2,1)} %w_self_hbm.1, bf16[512,512]{1,0:T(8,128)(2,1)} %w_neigh_hbm.1, bf16[1,1,8,3,128,128]{5,4,3,2,1,0:T(8,128)(2,1)} %weights_hbm.1, s32[1,3,1,8]{3,2,1,0:T(1,128)} %bitcast.1, s32[1,1,8]{2,1,0:T(1,128)} %counts_hbm.1), custom_call_target="tpu_custom_call" | custom-call | flops 671088640 | bytes 1310720 | tf_op jit(solution)/shard_map/refresh/pallas_call | solution.py:192
  25.4 1.6 %copy.8 = bf16[128,512]{1,0:T(8,128)(2,1)} copy(bf16[128,512]{1,0:T(8,128)(2,1)} %refresh.1) | data formatting | bytes 262144

commit v3 on v2

--- a/solution.py
+++ b/solution.py
@@ -14,8 +14,8 @@
 def refresh_kernel(
     blocks, members, stale_hbm, w_self_hbm, w_neigh_hbm, weights_hbm, places_hbm, counts_hbm,
     out_ref,
-    places_ref, counts_ref, w_self, w_neigh, weights, adjacency, gathered, partial, arrived, deg_send, deg_recv, total,
-    load_sem, g_send, g_recv, f_send, f_recv, p_send, p_recv, d_send, d_recv,
+    places_ref, counts_ref, w_self, w_neigh, weights, adjacency, gathered, partial, arrived, deg_send, deg_recv, relayed, total,
+    load_sem, g_send, g_recv, f_send, f_recv, p_send, p_recv, d_send, d_recv, r_recv,
 ):
     own, width = stale_hbm.shape
     cap, tile = weights_hbm.shape[3], weights_hbm.shape[4]
@@ -71,6 +71,62 @@
             send_sem=p_send.at[h, d - 1], recv_sem=p_recv.at[h, d - 1],
             device_id=member_at(d), device_id_type=MESH)
 
+    relaying = members >= 3
+    def to_relay(h, side):
+        d, helper = (members - 1, 1) if side == 0 else (1, members - 2)
+        return pltpu.make_async_remote_copy(
+            src_ref=partial.at[h, d], dst_ref=relayed.at[side, h],
+            send_sem=p_send.at[h, d - 1], recv_sem=r_recv.at[side, h],
+            device_id={"rep": helper}, device_id_type=MESH)
+
+    def ends_at(d):
+        found = []
+        if relaying and d == members - 1:
+            found.append((0, my_rep == 0))
+        if relaying and d == 1:
+            found.append((1, my_rep == members - 1))
+        return found
+
+    def helps_at(d):
+        found = []
+        if relaying and d == members - 2:
+            found.append((0, my_rep == 1))
+        if relaying and d == 2:
+            found.append((1, my_rep == members - 2))
+        return found
+
+    def send_sums(h, d):
+        direct = None
+        for side, here in ends_at(d):
+            pl.when(here)(lambda side=side: to_relay(h, side).start())
+        for side, here in ends_at(d) + helps_at(d):
+            direct = jnp.logical_not(here) if direct is None else direct & jnp.logical_not(here)
+        if direct is None:
+            to_member(h, d).start()
+        else:
+            pl.when(direct)(lambda: to_member(h, d).start())
+
+    def help_ends(h):
+        for d in range(1, members):
+            for side, here in helps_at(d):
+                @pl.when(here)
+                def _(d=d, side=side):
+                    to_relay(h, side).wait_recv()
+                    both = partial[h, d].astype(jnp.float32) + relayed[side, h].astype(jnp.float32)
+                    partial[h, d] = both.astype(jnp.bfloat16)
+                    to_member(h, d).start()
+
+    def wait_sums(h, d):
+        spared = None
+        if relaying and d == members - 1:
+            spared = my_rep == members - 1
+        if relaying and d == 1:
+            spared = my_rep == 0
+        if spared is None:
+            to_member(h, d).wait_recv()
+        else:
+            pl.when(jnp.logical_not(spared))(lambda: to_member(h, d).wait_recv())
+
     def degree_to(d):
         return pltpu.make_async_remote_copy(
             src_ref=deg_send.at[d], dst_ref=deg_recv.at[d - 1],
@@ -80,11 +136,16 @@
     for copy in own_loads:
         copy.wait()
     pl.semaphore_wait(barrier, len(peers))
-    for h in range(CHUNKS):
-        for o in range(1, chips):
-            to_chip(h, o).start()
-        to_pair(h, 0).start()
-
+    for o in range(1, chips):
+        to_chip(0, o).start()
+    to_pair(0, 0).start()
+
+    if relaying:
+        for end, d in ((members - 1, members - 1), (0, 1)):
+            @pl.when(my_rep == end)
+            def _(d=d):
+                for h in range(CHUNKS):
+                    arrived[h, d - 1] = jnp.zeros_like(arrived[h, d - 1])
     weights[blocks] = jnp.zeros_like(weights[blocks])
 
     place_load.wait()
@@ -120,6 +181,12 @@
 
     group = min(members, max(1, 512 // own))
     for h in range(CHUNKS):
+        if h + 1 < CHUNKS:
+            for o in range(1, chips):
+                to_chip(h, o).wait_send()
+            for o in range(1, chips):
+                to_chip(h + 1, o).start()
+            to_pair(h + 1, 0).start()
         for o in range(1, chips):
             to_chip(h, o).wait_recv()
             to_pair(h, o).start()
@@ -132,7 +199,9 @@
                            preferred_element_type=jnp.float32).astype(jnp.bfloat16)
             partial[h, first:last] = sums.reshape(last - first, own, chunk)
             for d in range(max(first, 1), last):
-                to_member(h, d).start()
+                send_sums(h, d)
+        if h > 0:
+            help_ends(h - 1)
         if h == 0:
             ones = jnp.ones((16, blocks * own), jnp.bfloat16)
             for d in range(members):
@@ -142,6 +211,7 @@
             for d in range(1, members):
                 degree_to(d).start()
 
+    help_ends(CHUNKS - 1)
     self_load.wait()
     total[...] = jnp.dot(gathered[0, 0], w_self[0:chunk, :], preferred_element_type=jnp.float32)
     for h in range(1, CHUNKS):
@@ -156,7 +226,7 @@
     for h in range(CHUNKS):
         summed = partial[h, 0].astype(jnp.float32)
         for d in range(1, members):
-            to_member(h, d).wait_recv()
+            wait_sums(h, d)
             summed = summed + arrived[h, d - 1].astype(jnp.float32)
         own_rows = gathered[h, 0].astype(jnp.float32)
         mean = ((own_rows + summed) * inverse).astype(jnp.bfloat16)
@@ -167,8 +237,9 @@
     out_ref[...] = (active * scale).astype(out_ref.dtype)
 
     for h in range(CHUNKS):
-        for o in range(1, chips):
-            to_chip(h, o).wait_send()
+        if h == CHUNKS - 1:
+            for o in range(1, chips):
+                to_chip(h, o).wait_send()
         for o in range(chips):
             to_pair(h, o).wait_send()
         for d in range(1, members):
@@ -206,6 +277,7 @@
             pltpu.VMEM((CHUNKS, members - 1, own, chunk), bf16),
             pltpu.VMEM((members, 16, own), bf16),
             pltpu.VMEM((members - 1, 16, own), bf16),
+            pltpu.VMEM((2, CHUNKS, own, chunk), bf16),
             pltpu.VMEM((own, width), f32),
             dma((CHUNKS + 5,)),
             dma((CHUNKS, chips)),
@@ -216,6 +288,7 @@
             dma((CHUNKS, members - 1)),
             dma((members - 1,)),
             dma((members - 1,)),
+            dma((2, CHUNKS)),
         ],
         compiler_params=pltpu.CompilerParams(
             collective_id=0, has_side_effects=True, vmem_limit_bytes=60 * 1024 * 1024),

time: 27.1 us -> 28.3 us (1.044)
  Pallas kernels: 25.4 us -> 26.6 us
    pallas_call x1, Pallas kernels: 25.4 us -> 26.6 us  [on_device(): pl.pallas_call(functools.partial(refresh_kernel, blocks, members), out_sh...]
where the time goes in v3:
time: 28.3 us; the launch traced here: 28.1 us
  Pallas kernels  26.6 us (94%)
  local copies, waits for them, and re-layouts  1.57 us (6%)
    pallas_call x1, Pallas kernels, on_device(): pl.pallas_call(functools.partial(refresh_kernel, blocks, members), out_sh...  26.6 us
    unnamed x1, local copies, waits for them, and re-layouts  1.57 us

profile of v3, /device:TPU:0, one launch (start us, length us, event | category | flops | bytes accessed | tf_op | source)
XLA Modules:
  0.0 28.1 jit_solution(9326462579352805182)
XLA Ops:
  0.0 26.6 %refresh.1 = bf16[128,512]{1,0:T(8,128)(2,1)} custom-call(bf16[128,512]{1,0:T(8,128)(2,1)} %stale_hbm.1, bf16[512,512]{1,0:T(8,128)(2,1)} %w_self_hbm.1, bf16[512,512]{1,0:T(8,128)(2,1)} %w_neigh_hbm.1, bf16[1,1,8,3,128,128]{5,4,3,2,1,0:T(8,128)(2,1)} %weights_hbm.1, s32[1,3,1,8]{3,2,1,0:T(1,128)} %bitcast.1, s32[1,1,8]{2,1,0:T(1,128)} %counts_hbm.1), custom_call_target="tpu_custom_call" | custom-call | flops 671088640 | bytes 1310720 | tf_op jit(solution)/shard_map/refresh/pallas_call | solution.py:263
  26.6 1.6 %copy.8 = bf16[128,512]{1,0:T(8,128)(2,1)} copy(bf16[128,512]{1,0:T(8,128)(2,1)} %refresh.1) | data formatting | bytes 262144

commit v4 on v3

--- a/solution.py
+++ b/solution.py
@@ -95,10 +95,12 @@
             found.append((1, my_rep == members - 2))
         return found
 
+    def relay_sums(h, d):
+        for side, here in ends_at(d):
+            pl.when(here)(lambda side=side: to_relay(h, side).start())
+
     def send_sums(h, d):
         direct = None
-        for side, here in ends_at(d):
-            pl.when(here)(lambda side=side: to_relay(h, side).start())
         for side, here in ends_at(d) + helps_at(d):
             direct = jnp.logical_not(here) if direct is None else direct & jnp.logical_not(here)
         if direct is None:
@@ -179,17 +181,31 @@
         def _(slot):
             place_tiles(slot)
 
-    group = min(members, max(1, 512 // own))
-    for h in range(CHUNKS):
-        if h + 1 < CHUNKS:
-            for o in range(1, chips):
-                to_chip(h, o).wait_send()
-            for o in range(1, chips):
-                to_chip(h + 1, o).start()
-            to_pair(h + 1, 0).start()
+    ones = jnp.ones((blocks * own, own), jnp.bfloat16)
+    for d in range(members):
+        row_sums = jnp.dot(adjacency[d * own:(d + 1) * own, :], ones,
+                           preferred_element_type=jnp.float32)
+        deg_send[d] = jnp.transpose(row_sums)[0:16].astype(jnp.bfloat16)
+    for d in range(1, members):
+        degree_to(d).start()
+
+    for o in range(1, chips):
+        to_chip(0, o).wait_send()
+    for h in range(1, CHUNKS):
+        for o in range(1, chips):
+            to_chip(h, o).start()
+        to_pair(h, 0).start()
+
+    def forward(h):
         for o in range(1, chips):
             to_chip(h, o).wait_recv()
             to_pair(h, o).start()
+
+    forward(0)
+    group = min(members, max(1, 512 // own))
+    for h in range(CHUNKS):
+        if 0 < h < CHUNKS - 1:
+            forward(h + 1)
         for o in range(chips):
             to_pair(h, o).wait_recv()
         sources = gathered[h].reshape(blocks * own, chunk)
@@ -199,24 +215,20 @@
                            preferred_element_type=jnp.float32).astype(jnp.bfloat16)
             partial[h, first:last] = sums.reshape(last - first, own, chunk)
             for d in range(max(first, 1), last):
+                relay_sums(h, d)
+            for d in range(max(first, 1), last):
                 send_sums(h, d)
         if h > 0:
             help_ends(h - 1)
-        if h == 0:
-            ones = jnp.ones((16, blocks * own), jnp.bfloat16)
-            for d in range(members):
-                deg_send[d] = lax.dot_general(
-                    ones, adjacency[d * own:(d + 1) * own, :], (((1,), (1,)), ((), ())),
-                    preferred_element_type=jnp.float32).astype(jnp.bfloat16)
-            for d in range(1, members):
-                degree_to(d).start()
-
-    help_ends(CHUNKS - 1)
+        elif CHUNKS > 1:
+            forward(1)
+
     self_load.wait()
     total[...] = jnp.dot(gathered[0, 0], w_self[0:chunk, :], preferred_element_type=jnp.float32)
     for h in range(1, CHUNKS):
         total[...] += jnp.dot(gathered[h, 0], w_self[h * chunk:(h + 1) * chunk, :],
                               preferred_element_type=jnp.float32)
+    help_ends(CHUNKS - 1)
     degree = deg_send[0].astype(jnp.float32)
     for d in range(1, members):
         degree_to(d).wait_recv()
@@ -237,8 +249,8 @@
     out_ref[...] = (active * scale).astype(out_ref.dtype)
 
     for h in range(CHUNKS):
-        if h == CHUNKS - 1:
-            for o in range(1, chips):
+        for o in range(1, chips):
+            if h > 0:
                 to_chip(h, o).wait_send()
         for o in range(chips):
             to_pair(h, o).wait_send()

time: 28.3 us -> 27.1 us (0.958)
  Pallas kernels: 26.6 us -> 25.4 us
    pallas_call x1, Pallas kernels: 26.6 us -> 25.4 us  [on_device(): pl.pallas_call(functools.partial(refresh_kernel, blocks, members), out_sh...]
where the time goes in v4:
time: 27.1 us; the launch traced here: 27 us
  Pallas kernels  25.4 us (94%)
  local copies, waits for them, and re-layouts  1.57 us (6%)
    pallas_call x1, Pallas kernels, on_device(): pl.pallas_call(functools.partial(refresh_kernel, blocks, members), out_sh...  25.4 us
    unnamed x1, local copies, waits for them, and re-layouts  1.57 us

profile of v4, /device:TPU:0, one launch (start us, length us, event | category | flops | bytes accessed | tf_op | source)
XLA Modules:
  0.0 27.0 jit_solution(14264038562639786494)
XLA Ops:
  0.0 25.4 %refresh.1 = bf16[128,512]{1,0:T(8,128)(2,1)} custom-call(bf16[128,512]{1,0:T(8,128)(2,1)} %stale_hbm.1, bf16[512,512]{1,0:T(8,128)(2,1)} %w_self_hbm.1, bf16[512,512]{1,0:T(8,128)(2,1)} %w_neigh_hbm.1, bf16[1,1,8,3,128,128]{5,4,3,2,1,0:T(8,128)(2,1)} %weights_hbm.1, s32[1,3,1,8]{3,2,1,0:T(1,128)} %bitcast.1, s32[1,1,8]{2,1,0:T(1,128)} %counts_hbm.1), custom_call_target="tpu_custom_call" | custom-call | flops 671088640 | bytes 1310720 | tf_op jit(solution)/shard_map/refresh/pallas_call | solution.py:275
  25.4 1.6 %copy.8 = bf16[128,512]{1,0:T(8,128)(2,1)} copy(bf16[128,512]{1,0:T(8,128)(2,1)} %refresh.1) | data formatting | bytes 262144

commit v5 on v4

--- a/solution.py
+++ b/solution.py
@@ -40,8 +40,16 @@
     neigh_load = load(CHUNKS + 4, w_neigh_hbm, w_neigh)
 
     pair = {"blk": chip * 2 + 1 - core}
+    def across(offset, sign):
+        if chips & (chips - 1):
+            return (chip + chips + sign * offset) % chips
+        other, bit = 0, 1
+        while bit < chips:
+            other = other + (chip // bit % 2 + offset // bit % 2) % 2 * bit
+            bit *= 2
+        return other
     def chip_at(offset):
-        return {"blk": ((chip + offset) % chips) * 2 + core}
+        return {"blk": across(offset, 1) * 2 + core}
     def member_at(offset):
         return {"rep": (my_rep + offset) % members}
 
@@ -55,13 +63,14 @@
 
     def to_chip(h, o):
         return pltpu.make_async_remote_copy(
-            src_ref=gathered.at[h, 0], dst_ref=gathered.at[h, 2 * o],
+            src_ref=stale_hbm.at[:, pl.ds(h * chunk, chunk)], dst_ref=gathered.at[h, 2 * o],
             send_sem=g_send.at[h, o], recv_sem=g_recv.at[h, o],
             device_id=chip_at(o), device_id_type=MESH)
 
     def to_pair(h, o):
-        return pltpu.make_async_remote_copy(
-            src_ref=gathered.at[h, 2 * o], dst_ref=gathered.at[h, 2 * o + 1],
+        source = stale_hbm.at[:, pl.ds(h * chunk, chunk)] if o == 0 else gathered.at[h, 2 * o]
+        return pltpu.make_async_remote_copy(
+            src_ref=source, dst_ref=gathered.at[h, 2 * o + 1],
             send_sem=f_send.at[h, o], recv_sem=f_recv.at[h, o],
             device_id=pair, device_id_type=MESH)
 
@@ -71,7 +80,8 @@
             send_sem=p_send.at[h, d - 1], recv_sem=p_recv.at[h, d - 1],
             device_id=member_at(d), device_id_type=MESH)
 
-    relaying = members >= 3
+    def relaying(h):
+        return members >= 3 and h < CHUNKS - 1
     def to_relay(h, side):
         d, helper = (members - 1, 1) if side == 0 else (1, members - 2)
         return pltpu.make_async_remote_copy(
@@ -79,29 +89,29 @@
             send_sem=p_send.at[h, d - 1], recv_sem=r_recv.at[side, h],
             device_id={"rep": helper}, device_id_type=MESH)
 
-    def ends_at(d):
+    def ends_at(h, d):
         found = []
-        if relaying and d == members - 1:
+        if relaying(h) and d == members - 1:
             found.append((0, my_rep == 0))
-        if relaying and d == 1:
+        if relaying(h) and d == 1:
             found.append((1, my_rep == members - 1))
         return found
 
-    def helps_at(d):
+    def helps_at(h, d):
         found = []
-        if relaying and d == members - 2:
+        if relaying(h) and d == members - 2:
             found.append((0, my_rep == 1))
-        if relaying and d == 2:
+        if relaying(h) and d == 2:
             found.append((1, my_rep == members - 2))
         return found
 
     def relay_sums(h, d):
-        for side, here in ends_at(d):
+        for side, here in ends_at(h, d):
             pl.when(here)(lambda side=side: to_relay(h, side).start())
 
     def send_sums(h, d):
         direct = None
-        for side, here in ends_at(d) + helps_at(d):
+        for side, here in ends_at(h, d) + helps_at(h, d):
             direct = jnp.logical_not(here) if direct is None else direct & jnp.logical_not(here)
         if direct is None:
             to_member(h, d).start()
@@ -110,7 +120,7 @@
 
     def help_ends(h):
         for d in range(1, members):
-            for side, here in helps_at(d):
+            for side, here in helps_at(h, d):
                 @pl.when(here)
                 def _(d=d, side=side):
                     to_relay(h, side).wait_recv()
@@ -120,9 +130,9 @@
 
     def wait_sums(h, d):
         spared = None
-        if relaying and d == members - 1:
+        if relaying(h) and d == members - 1:
             spared = my_rep == members - 1
-        if relaying and d == 1:
+        if relaying(h) and d == 1:
             spared = my_rep == 0
         if spared is None:
             to_member(h, d).wait_recv()
@@ -135,26 +145,25 @@
             send_sem=d_send.at[d - 1], recv_sem=d_recv.at[d - 1],
             device_id=member_at(d), device_id_type=MESH)
 
-    for copy in own_loads:
-        copy.wait()
     pl.semaphore_wait(barrier, len(peers))
-    for o in range(1, chips):
+    for o in reversed(range(1, chips)):
         to_chip(0, o).start()
     to_pair(0, 0).start()
 
-    if relaying:
+    if members >= 3:
         for end, d in ((members - 1, members - 1), (0, 1)):
             @pl.when(my_rep == end)
             def _(d=d):
                 for h in range(CHUNKS):
-                    arrived[h, d - 1] = jnp.zeros_like(arrived[h, d - 1])
+                    if relaying(h):
+                        arrived[h, d - 1] = jnp.zeros_like(arrived[h, d - 1])
     weights[blocks] = jnp.zeros_like(weights[blocks])
 
     place_load.wait()
     count_load.wait()
     tile_load.wait()
     def place_tiles(slot):
-        source = ((chip + chips - slot // 2) % chips) * 2 + (core + slot % 2) % 2
+        source = across(slot // 2, -1) * 2 + (core + slot % 2) % 2
         live = counts_ref[0, 0, source]
         spots = [
             jnp.where(k < live, places_ref[0, k, 0, source], -1) for k in range(cap)
@@ -192,7 +201,7 @@
     for o in range(1, chips):
         to_chip(0, o).wait_send()
     for h in range(1, CHUNKS):
-        for o in range(1, chips):
+        for o in reversed(range(1, chips)):
             to_chip(h, o).start()
         to_pair(h, 0).start()
 
@@ -201,6 +210,8 @@
             to_chip(h, o).wait_recv()
             to_pair(h, o).start()
 
+    for copy in own_loads:
+        copy.wait()
     forward(0)
     group = min(members, max(1, 512 // own))
     for h in range(CHUNKS):
@@ -274,7 +285,7 @@
     flops = 2 * own * width * (members * own * blocks + 2 * width)
     return pl.pallas_call(
         functools.partial(refresh_kernel, blocks, members),
-        out_shape=jax.ShapeDtypeStruct((own, width), bf16),
+        out_shape=pltpu.VMEM((own, width), bf16),
         in_specs=[hbm] * 6,
         out_specs=vmem,
         scratch_shapes=[

time: 27.1 us -> 25.7 us (0.948)
  local copies, waits for them, and re-layouts: 1.57 us -> 0.66 us
  Pallas kernels: 25.4 us -> 24.9 us
    unnamed x1, local copies, waits for them, and re-layouts: 1.57 us -> 0.66 us
    pallas_call x1, Pallas kernels: 25.4 us -> 24.9 us  [on_device(): pl.pallas_call(functools.partial(refresh_kernel, blocks, members), out_sh...]
where the time goes in v5:
time: 25.7 us; the launch traced here: 25.6 us
  Pallas kernels  24.9 us (97%)
  local copies, waits for them, and re-layouts  0.66 us (3%)
    pallas_call x1, Pallas kernels, on_device(): pl.pallas_call(functools.partial(refresh_kernel, blocks, members), out_sh...  24.9 us
    unnamed x1, local copies, waits for them, and re-layouts  0.66 us

profile of v5, /device:TPU:0, one launch (start us, length us, event | category | flops | bytes accessed | tf_op | source)
XLA Modules:
  0.0 25.6 jit_solution(13957134476125397870)
XLA Ops:
  0.0 24.9 %refresh.1 = bf16[128,512]{1,0:T(8,128)(2,1)S(1)} custom-call(bf16[128,512]{1,0:T(8,128)(2,1)} %stale_hbm.1, bf16[512,512]{1,0:T(8,128)(2,1)} %w_self_hbm.1, bf16[512,512]{1,0:T(8,128)(2,1)} %w_neigh_hbm.1, bf16[1,1,8,3,128,128]{5,4,3,2,1,0:T(8,128)(2,1)} %weights_hbm.1, s32[1,3,1,8]{3,2,1,0:T(1,128)} %bitcast.1, s32[1,1,8]{2,1,0:T(1,128)} %counts_hbm.1), custom_call_target="tpu_custom_call" | custom-call | flops 671088640 | bytes 1310720 | tf_op jit(solution)/shard_map/refresh/pallas_call | solution.py:286
  24.9 0.7 %copy.8 = bf16[128,512]{1,0:T(8,128)(2,1)} copy(bf16[128,512]{1,0:T(8,128)(2,1)S(1)} %refresh.1) | data formatting | bytes 262144

commit v6 on v5

--- a/solution.py
+++ b/solution.py
@@ -58,7 +58,7 @@
     peers += [chip_at(o) for o in range(1, chips)] + [pair]
     for peer in peers:
         pl.semaphore_signal(barrier, inc=1, device_id=peer, device_id_type=MESH)
-    for copy in own_loads + [place_load, count_load, tile_load, self_load, neigh_load]:
+    for copy in [place_load, count_load, tile_load]:
         copy.start()
 
     def to_chip(h, o):
@@ -149,6 +149,8 @@
     for o in reversed(range(1, chips)):
         to_chip(0, o).start()
     to_pair(0, 0).start()
+    for copy in own_loads + [self_load, neigh_load]:
+        copy.start()
 
     if members >= 3:
         for end, d in ((members - 1, members - 1), (0, 1)):
@@ -227,8 +229,15 @@
             partial[h, first:last] = sums.reshape(last - first, own, chunk)
             for d in range(max(first, 1), last):
                 relay_sums(h, d)
-            for d in range(max(first, 1), last):
-                send_sums(h, d)
+            low = my_rep * 2 < members
+            @pl.when(low)
+            def _(h=h, first=first, last=last):
+                for d in reversed(range(max(first, 1), last)):
+                    send_sums(h, d)
+            @pl.when(jnp.logical_not(low))
+            def _(h=h, first=first, last=last):
+                for d in range(max(first, 1), last):
+                    send_sums(h, d)
         if h > 0:
             help_ends(h - 1)
         elif CHUNKS > 1:

time: 25.7 us -> 25.7 us (level)
  no operation moved by 1% of the time
where the time goes in v6:
time: 25.7 us; the launch traced here: 25.6 us
  Pallas kernels  24.9 us (97%)
  local copies, waits for them, and re-layouts  0.66 us (3%)
    pallas_call x1, Pallas kernels, on_device(): pl.pallas_call(functools.partial(refresh_kernel, blocks, members), out_sh...  24.9 us
    unnamed x1, local copies, waits for them, and re-layouts  0.66 us

profile of v6, /device:TPU:0, one launch (start us, length us, event | category | flops | bytes accessed | tf_op | source)
XLA Modules:
  0.0 25.6 jit_solution(13595003684141935332)
XLA Ops:
  0.0 24.9 %refresh.1 = bf16[128,512]{1,0:T(8,128)(2,1)S(1)} custom-call(bf16[128,512]{1,0:T(8,128)(2,1)} %stale_hbm.1, bf16[512,512]{1,0:T(8,128)(2,1)} %w_self_hbm.1, bf16[512,512]{1,0:T(8,128)(2,1)} %w_neigh_hbm.1, bf16[1,1,8,3,128,128]{5,4,3,2,1,0:T(8,128)(2,1)} %weights_hbm.1, s32[1,3,1,8]{3,2,1,0:T(1,128)} %bitcast.1, s32[1,1,8]{2,1,0:T(1,128)} %counts_hbm.1), custom_call_target="tpu_custom_call" | custom-call | flops 671088640 | bytes 1310720 | tf_op jit(solution)/shard_map/refresh/pallas_call | solution.py:295
  24.9 0.7 %copy.8 = bf16[128,512]{1,0:T(8,128)(2,1)} copy(bf16[128,512]{1,0:T(8,128)(2,1)S(1)} %refresh.1) | data formatting | bytes 262144

commit v7 on v6

--- a/solution.py
+++ b/solution.py
@@ -8,7 +8,7 @@
 from jax.sharding import PartitionSpec as P
 
 MESH = pl.DeviceIdType.MESH
-CHUNKS = 4
+CHUNKS = 2
 
 
 def refresh_kernel(

time: 25.7 us -> 25.7 us (level)
  no operation moved by 1% of the time
where the time goes in v7:
time: 25.7 us; the launch traced here: 25.5 us
  Pallas kernels  24.8 us (96%)
  local copies, waits for them, and re-layouts  0.66 us (3%)
    pallas_call x1, Pallas kernels, on_device(): pl.pallas_call(functools.partial(refresh_kernel, blocks, members), out_sh...  24.8 us
    unnamed x1, local copies, waits for them, and re-layouts  0.66 us

profile of v7, /device:TPU:0, one launch (start us, length us, event | category | flops | bytes accessed | tf_op | source)
XLA Modules:
  0.0 25.5 jit_solution(6869357721763967413)
XLA Ops:
  0.0 24.8 %refresh.1 = bf16[128,512]{1,0:T(8,128)(2,1)S(1)} custom-call(bf16[128,512]{1,0:T(8,128)(2,1)} %stale_hbm.1, bf16[512,512]{1,0:T(8,128)(2,1)} %w_self_hbm.1, bf16[512,512]{1,0:T(8,128)(2,1)} %w_neigh_hbm.1, bf16[1,1,8,3,128,128]{5,4,3,2,1,0:T(8,128)(2,1)} %weights_hbm.1, s32[1,3,1,8]{3,2,1,0:T(1,128)} %bitcast.1, s32[1,1,8]{2,1,0:T(1,128)} %counts_hbm.1), custom_call_target="tpu_custom_call" | custom-call | flops 671088640 | bytes 1310720 | tf_op jit(solution)/shard_map/refresh/pallas_call | solution.py:295
  24.9 0.7 %copy.8 = bf16[128,512]{1,0:T(8,128)(2,1)} copy(bf16[128,512]{1,0:T(8,128)(2,1)S(1)} %refresh.1) | data formatting | bytes 262144

commit v8 on v7

--- a/solution.py
+++ b/solution.py
@@ -8,7 +8,13 @@
 from jax.sharding import PartitionSpec as P
 
 MESH = pl.DeviceIdType.MESH
-CHUNKS = 2
+QUARTERS = (1, 2, 1)
+CHUNKS = len(QUARTERS)
+
+
+def chunk_of(width, h):
+    unit = width // sum(QUARTERS)
+    return sum(QUARTERS[:h]) * unit, QUARTERS[h] * unit
 
 
 def refresh_kernel(
@@ -21,16 +27,18 @@
     cap, tile = weights_hbm.shape[3], weights_hbm.shape[4]
     col_tiles = own // tile
     chips = blocks // 2
-    chunk = width // CHUNKS
     my_blk = lax.axis_index("blk")
     my_rep = lax.axis_index("rep")
     chip, core = my_blk // 2, my_blk % 2
 
+    def columns(h):
+        return pl.ds(*chunk_of(width, h))
+
     def load(slot, source, target):
         return pltpu.make_async_copy(source, target, load_sem.at[slot])
 
     own_loads = [
-        load(h, stale_hbm.at[:, pl.ds(h * chunk, chunk)], gathered.at[h, 0])
+        load(h, stale_hbm.at[:, columns(h)], gathered[h].at[0])
         for h in range(CHUNKS)
     ]
     place_load = load(CHUNKS, places_hbm, places_ref)
@@ -63,20 +71,20 @@
 
     def to_chip(h, o):
         return pltpu.make_async_remote_copy(
-            src_ref=stale_hbm.at[:, pl.ds(h * chunk, chunk)], dst_ref=gathered.at[h, 2 * o],
+            src_ref=stale_hbm.at[:, columns(h)], dst_ref=gathered[h].at[2 * o],
             send_sem=g_send.at[h, o], recv_sem=g_recv.at[h, o],
             device_id=chip_at(o), device_id_type=MESH)
 
     def to_pair(h, o):
-        source = stale_hbm.at[:, pl.ds(h * chunk, chunk)] if o == 0 else gathered.at[h, 2 * o]
-        return pltpu.make_async_remote_copy(
-            src_ref=source, dst_ref=gathered.at[h, 2 * o + 1],
+        source = stale_hbm.at[:, columns(h)] if o == 0 else gathered[h].at[2 * o]
+        return pltpu.make_async_remote_copy(
+            src_ref=source, dst_ref=gathered[h].at[2 * o + 1],
             send_sem=f_send.at[h, o], recv_sem=f_recv.at[h, o],
             device_id=pair, device_id_type=MESH)
 
     def to_member(h, d):
         return pltpu.make_async_remote_copy(
-            src_ref=partial.at[h, d], dst_ref=arrived.at[h, d - 1],
+            src_ref=partial[h].at[d], dst_ref=arrived[h].at[d - 1],
             send_sem=p_send.at[h, d - 1], recv_sem=p_recv.at[h, d - 1],
             device_id=member_at(d), device_id_type=MESH)
 
@@ -85,7 +93,7 @@
     def to_relay(h, side):
         d, helper = (members - 1, 1) if side == 0 else (1, members - 2)
         return pltpu.make_async_remote_copy(
-            src_ref=partial.at[h, d], dst_ref=relayed.at[side, h],
+            src_ref=partial[h].at[d], dst_ref=relayed[h].at[side],
             send_sem=p_send.at[h, d - 1], recv_sem=r_recv.at[side, h],
             device_id={"rep": helper}, device_id_type=MESH)
 
@@ -124,8 +132,8 @@
                 @pl.when(here)
                 def _(d=d, side=side):
                     to_relay(h, side).wait_recv()
-                    both = partial[h, d].astype(jnp.float32) + relayed[side, h].astype(jnp.float32)
-                    partial[h, d] = both.astype(jnp.bfloat16)
+                    both = partial[h][d].astype(jnp.float32) + relayed[h][side].astype(jnp.float32)
+                    partial[h][d] = both.astype(jnp.bfloat16)
                     to_member(h, d).start()
 
     def wait_sums(h, d):
@@ -158,12 +166,19 @@
             def _(d=d):
                 for h in range(CHUNKS):
                     if relaying(h):
-                        arrived[h, d - 1] = jnp.zeros_like(arrived[h, d - 1])
+                        arrived[h][d - 1] = jnp.zeros_like(arrived[h][d - 1])
     weights[blocks] = jnp.zeros_like(weights[blocks])
 
     place_load.wait()
     count_load.wait()
     tile_load.wait()
+    for o in range(1, chips):
+        to_chip(0, o).wait_send()
+    for h in range(1, CHUNKS):
+        for o in reversed(range(1, chips)):
+            to_chip(h, o).start()
+        to_pair(h, 0).start()
+
     def place_tiles(slot):
         source = across(slot // 2, -1) * 2 + (core + slot % 2) % 2
         live = counts_ref[0, 0, source]
@@ -192,6 +207,14 @@
         def _(slot):
             place_tiles(slot)
 
+    def forward(h):
+        for o in range(1, chips):
+            to_chip(h, o).wait_recv()
+            to_pair(h, o).start()
+
+    for copy in own_loads:
+        copy.wait()
+    forward(0)
     ones = jnp.ones((blocks * own, own), jnp.bfloat16)
     for d in range(members):
         row_sums = jnp.dot(adjacency[d * own:(d + 1) * own, :], ones,
@@ -200,33 +223,19 @@
     for d in range(1, members):
         degree_to(d).start()
 
-    for o in range(1, chips):
-        to_chip(0, o).wait_send()
-    for h in range(1, CHUNKS):
-        for o in reversed(range(1, chips)):
-            to_chip(h, o).start()
-        to_pair(h, 0).start()
-
-    def forward(h):
-        for o in range(1, chips):
-            to_chip(h, o).wait_recv()
-            to_pair(h, o).start()
-
-    for copy in own_loads:
-        copy.wait()
-    forward(0)
     group = min(members, max(1, 512 // own))
     for h in range(CHUNKS):
         if 0 < h < CHUNKS - 1:
             forward(h + 1)
         for o in range(chips):
             to_pair(h, o).wait_recv()
-        sources = gathered[h].reshape(blocks * own, chunk)
+        size = chunk_of(width, h)[1]
+        sources = gathered[h][...].reshape(blocks * own, size)
         for first in range(0, members, group):
             last = min(first + group, members)
             sums = jnp.dot(adjacency[first * own:last * own, :], sources,
                            preferred_element_type=jnp.float32).astype(jnp.bfloat16)
-            partial[h, first:last] = sums.reshape(last - first, own, chunk)
+            partial[h][first:last] = sums.reshape(last - first, own, size)
             for d in range(max(first, 1), last):
                 relay_sums(h, d)
             low = my_rep * 2 < members
@@ -244,9 +253,9 @@
             forward(1)
 
     self_load.wait()
-    total[...] = jnp.dot(gathered[0, 0], w_self[0:chunk, :], preferred_element_type=jnp.float32)
+    total[...] = jnp.dot(gathered[0][0], w_self[columns(0), :], preferred_element_type=jnp.float32)
     for h in range(1, CHUNKS):
-        total[...] += jnp.dot(gathered[h, 0], w_self[h * chunk:(h + 1) * chunk, :],
+        total[...] += jnp.dot(gathered[h][0], w_self[columns(h), :],
                               preferred_element_type=jnp.float32)
     help_ends(CHUNKS - 1)
     degree = deg_send[0].astype(jnp.float32)
@@ -256,13 +265,13 @@
     inverse = jnp.transpose(jnp.broadcast_to(1.0 / (1.0 + degree[0:1]), (own, own)))[:, 0:1]
     neigh_load.wait()
     for h in range(CHUNKS):
-        summed = partial[h, 0].astype(jnp.float32)
+        summed = partial[h][0].astype(jnp.float32)
         for d in range(1, members):
             wait_sums(h, d)
-            summed = summed + arrived[h, d - 1].astype(jnp.float32)
-        own_rows = gathered[h, 0].astype(jnp.float32)
+            summed = summed + arrived[h][d - 1].astype(jnp.float32)
+        own_rows = gathered[h][0].astype(jnp.float32)
         mean = ((own_rows + summed) * inverse).astype(jnp.bfloat16)
-        total[...] += jnp.dot(mean, w_neigh[h * chunk:(h + 1) * chunk, :],
+        total[...] += jnp.dot(mean, w_neigh[columns(h), :],
                               preferred_element_type=jnp.float32)
     active = jnp.maximum(total[...], 0.0)
     scale = lax.rsqrt(jnp.mean(active * active, axis=-1, keepdims=True) + 1e-05)
@@ -286,7 +295,9 @@
     own, width = stale.shape
     cap, tile = tile_weights.shape[3], tile_weights.shape[4]
     chips = blocks // 2
-    chunk = width // CHUNKS
+    sizes = [chunk_of(width, h)[1] for h in range(CHUNKS)]
+    def buffers(count):
+        return tuple(pltpu.VMEM((count, own, size), bf16) for size in sizes)
     bf16, f32 = jnp.bfloat16, jnp.float32
     dma = pltpu.SemaphoreType.DMA
     vmem = pl.BlockSpec(memory_space=pltpu.VMEM)
@@ -304,12 +315,12 @@
             pltpu.VMEM(w_neigh.shape, bf16),
             pltpu.VMEM((blocks + 1, cap, tile, tile), bf16),
             pltpu.VMEM((members * own, blocks * own), bf16),
-            pltpu.VMEM((CHUNKS, blocks, own, chunk), bf16),
-            pltpu.VMEM((CHUNKS, members, own, chunk), bf16),
-            pltpu.VMEM((CHUNKS, members - 1, own, chunk), bf16),
+            buffers(blocks),
+            buffers(members),
+            buffers(members - 1),
             pltpu.VMEM((members, 16, own), bf16),
             pltpu.VMEM((members - 1, 16, own), bf16),
-            pltpu.VMEM((2, CHUNKS, own, chunk), bf16),
+            buffers(2),
             pltpu.VMEM((own, width), f32),
             dma((CHUNKS + 5,)),
             dma((CHUNKS, chips)),

time: 25.7 us -> 25.9 us (level)
  Pallas kernels: 24.8 us -> 25.1 us
    pallas_call x1, Pallas kernels: 24.8 us -> 25.1 us  [on_device(): pl.pallas_call(functools.partial(refresh_kernel, blocks, members), out_sh...]
where the time goes in v8:
time: 25.9 us; the launch traced here: 25.8 us
  Pallas kernels  25.1 us (97%)
  local copies, waits for them, and re-layouts  0.66 us (3%)
    pallas_call x1, Pallas kernels, on_device(): pl.pallas_call(functools.partial(refresh_kernel, blocks, members), out_sh...  25.1 us
    unnamed x1, local copies, waits for them, and re-layouts  0.66 us

profile of v8, /device:TPU:0, one launch (start us, length us, event | category | flops | bytes accessed | tf_op | source)
XLA Modules:
  0.0 25.8 jit_solution(3005381263939805224)
XLA Ops:
  0.0 25.1 %refresh.1 = bf16[128,512]{1,0:T(8,128)(2,1)S(1)} custom-call(bf16[128,512]{1,0:T(8,128)(2,1)} %stale_hbm.1, bf16[512,512]{1,0:T(8,128)(2,1)} %w_self_hbm.1, bf16[512,512]{1,0:T(8,128)(2,1)} %w_neigh_hbm.1, bf16[1,1,8,3,128,128]{5,4,3,2,1,0:T(8,128)(2,1)} %weights_hbm.1, s32[1,3,1,8]{3,2,1,0:T(1,128)} %bitcast.1, s32[1,1,8]{2,1,0:T(1,128)} %counts_hbm.1), custom_call_target="tpu_custom_call" | custom-call | flops 671088640 | bytes 1310720 | tf_op jit(solution)/shard_map/refresh/pallas_call | solution.py:306
  25.1 0.7 %copy.8 = bf16[128,512]{1,0:T(8,128)(2,1)} copy(bf16[128,512]{1,0:T(8,128)(2,1)S(1)} %refresh.1) | data formatting | bytes 262144

commit v9 on v8

--- a/solution.py
+++ b/solution.py
@@ -8,7 +8,7 @@
 from jax.sharding import PartitionSpec as P
 
 MESH = pl.DeviceIdType.MESH
-QUARTERS = (1, 2, 1)
+QUARTERS = (1, 1, 1, 1)
 CHUNKS = len(QUARTERS)
 
 
@@ -71,12 +71,13 @@
 
     def to_chip(h, o):
         return pltpu.make_async_remote_copy(
-            src_ref=stale_hbm.at[:, columns(h)], dst_ref=gathered[h].at[2 * o],
+            src_ref=stale_hbm.at[:, columns(h)] if h == 0 else gathered[h].at[0],
+            dst_ref=gathered[h].at[2 * o],
             send_sem=g_send.at[h, o], recv_sem=g_recv.at[h, o],
             device_id=chip_at(o), device_id_type=MESH)
 
     def to_pair(h, o):
-        source = stale_hbm.at[:, columns(h)] if o == 0 else gathered[h].at[2 * o]
+        source = stale_hbm.at[:, columns(h)] if h + o == 0 else gathered[h].at[2 * o]
         return pltpu.make_async_remote_copy(
             src_ref=source, dst_ref=gathered[h].at[2 * o + 1],
             send_sem=f_send.at[h, o], recv_sem=f_recv.at[h, o],
@@ -174,10 +175,14 @@
     tile_load.wait()
     for o in range(1, chips):
         to_chip(0, o).wait_send()
-    for h in range(1, CHUNKS):
+    for copy in own_loads:
+        copy.wait()
+    def spread(h):
         for o in reversed(range(1, chips)):
             to_chip(h, o).start()
         to_pair(h, 0).start()
+
+    spread(1)
 
     def place_tiles(slot):
         source = across(slot // 2, -1) * 2 + (core + slot % 2) % 2
@@ -212,9 +217,10 @@
             to_chip(h, o).wait_recv()
             to_pair(h, o).start()
 
-    for copy in own_loads:
-        copy.wait()
+    spread(2)
     forward(0)
+    for h in range(3, CHUNKS):
+        spread(h)
     ones = jnp.ones((blocks * own, own), jnp.bfloat16)
     for d in range(members):
         row_sums = jnp.dot(adjacency[d * own:(d + 1) * own, :], ones,

time: 25.9 us -> 25.8 us (level)
  no operation moved by 1% of the time
where the time goes in v9:
time: 25.8 us; the launch traced here: 25.6 us
  Pallas kernels  25 us (97%)
  local copies, waits for them, and re-layouts  0.66 us (3%)
    pallas_call x1, Pallas kernels, on_device(): pl.pallas_call(functools.partial(refresh_kernel, blocks, members), out_sh...  25 us
    unnamed x1, local copies, waits for them, and re-layouts  0.66 us

profile of v9, /device:TPU:0, one launch (start us, length us, event | category | flops | bytes accessed | tf_op | source)
XLA Modules:
  0.0 25.6 jit_solution(18269198388442358269)
XLA Ops:
  0.0 25.0 %refresh.1 = bf16[128,512]{1,0:T(8,128)(2,1)S(1)} custom-call(bf16[128,512]{1,0:T(8,128)(2,1)} %stale_hbm.1, bf16[512,512]{1,0:T(8,128)(2,1)} %w_self_hbm.1, bf16[512,512]{1,0:T(8,128)(2,1)} %w_neigh_hbm.1, bf16[1,1,8,3,128,128]{5,4,3,2,1,0:T(8,128)(2,1)} %weights_hbm.1, s32[1,3,1,8]{3,2,1,0:T(1,128)} %bitcast.1, s32[1,1,8]{2,1,0:T(1,128)} %counts_hbm.1), custom_call_target="tpu_custom_call" | custom-call | flops 671088640 | bytes 1310720 | tf_op jit(solution)/shard_map/refresh/pallas_call | solution.py:312
  25.0 0.7 %copy.8 = bf16[128,512]{1,0:T(8,128)(2,1)} copy(bf16[128,512]{1,0:T(8,128)(2,1)S(1)} %refresh.1) | data formatting | bytes 262144

commit v10 on v6

--- a/solution.py
+++ b/solution.py
@@ -81,7 +81,7 @@
             device_id=member_at(d), device_id_type=MESH)
 
     def relaying(h):
-        return members >= 3 and h < CHUNKS - 1
+        return members >= 3 and h < CHUNKS // 2
     def to_relay(h, side):
         d, helper = (members - 1, 1) if side == 0 else (1, members - 2)
         return pltpu.make_async_remote_copy(

time: 25.7 us -> 25.8 us (level)
  no operation moved by 1% of the time
where the time goes in v10:
time: 25.8 us; the launch traced here: 25.7 us
  Pallas kernels  25 us (97%)
  local copies, waits for them, and re-layouts  0.66 us (3%)
    pallas_call x1, Pallas kernels, on_device(): pl.pallas_call(functools.partial(refresh_kernel, blocks, members), out_sh...  25 us
    unnamed x1, local copies, waits for them, and re-layouts  0.66 us

profile of v10, /device:TPU:0, one launch (start us, length us, event | category | flops | bytes accessed | tf_op | source)
XLA Modules:
  0.0 25.7 jit_solution(302458698762684071)
XLA Ops:
  0.0 25.0 %refresh.1 = bf16[128,512]{1,0:T(8,128)(2,1)S(1)} custom-call(bf16[128,512]{1,0:T(8,128)(2,1)} %stale_hbm.1, bf16[512,512]{1,0:T(8,128)(2,1)} %w_self_hbm.1, bf16[512,512]{1,0:T(8,128)(2,1)} %w_neigh_hbm.1, bf16[1,1,8,3,128,128]{5,4,3,2,1,0:T(8,128)(2,1)} %weights_hbm.1, s32[1,3,1,8]{3,2,1,0:T(1,128)} %bitcast.1, s32[1,1,8]{2,1,0:T(1,128)} %counts_hbm.1), custom_call_target="tpu_custom_call" | custom-call | flops 671088640 | bytes 1310720 | tf_op jit(solution)/shard_map/refresh/pallas_call | solution.py:295
  25.0 0.7 %copy.8 = bf16[128,512]{1,0:T(8,128)(2,1)} copy(bf16[128,512]{1,0:T(8,128)(2,1)S(1)} %refresh.1) | data formatting | bytes 262144
